TPU v7x, 32 devices: a whole 2x2x4 slice. The times are simulated.
32 devices in a mesh: ctx: 8 (over z, y), fsdp: 4 (over x, core).
Axes of the slice: x: 2, y: 2, z: 4, core: 2. Of those that a mesh axis runs over, the one named last changes fastest.
Arguments:
- tokens: bfloat16 [4, 2048, 768], P('fsdp', 'ctx'), may hold values from -6 to 6
- cotangent: bfloat16 [4, 2048, 768], P('fsdp', 'ctx'), may hold values from -6 to 6
- lengths: int32 [4], P('fsdp'), may hold values from 512 to 2048, as said below
- pairing: int32 [16], replicated, may hold values from 0 to 15, as said below
- w_qkv: bfloat16 [768, 2304], P('fsdp'), may hold values from -0.21875 to 0.21875
- bias_q: bfloat16 [768], P('fsdp'), may hold values from -3 to 3
- bias_v: bfloat16 [768], P('fsdp'), may hold values from -3 to 3
- w_out: bfloat16 [768, 768], P('fsdp'), may hold values from -6 to 6
- bias_out: bfloat16 [768], P('fsdp'), may hold values from -3 to 3
- ln1_gain: bfloat16 [768], P('fsdp'), may hold values from 0.099609375 to 1.8984375
- ln1_bias: bfloat16 [768], P('fsdp'), may hold values from -3 to 3
- w_in: bfloat16 [768, 3072], P('fsdp'), may hold values from -0.21875 to 0.21875
- bias_in: bfloat16 [3072], P('fsdp'), may hold values from -3 to 3
- w_back: bfloat16 [3072, 768], P('fsdp'), may hold values from -0.109375 to 0.109375
- bias_back: bfloat16 [768], P('fsdp'), may hold values from -3 to 3
- ln2_gain: bfloat16 [768], P('fsdp'), may hold values from 0.099609375 to 1.8984375
- ln2_bias: bfloat16 [768], P('fsdp'), may hold values from -3 to 3
Outputs:
- output: float32 [4, 2048, 768], P('fsdp', 'ctx')
- token_grad: float32 [4, 2048, 768], P('fsdp', 'ctx')
- w_qkv_grad: float32 [768, 2304], P('fsdp')
- bias_q_grad: float32 [768], P('fsdp')
- bias_v_grad: float32 [768], P('fsdp')
- w_out_grad: float32 [768, 768], P('fsdp')
- bias_out_grad: float32 [768], P('fsdp')
- ln1_gain_grad: float32 [768], P('fsdp')
- ln1_bias_grad: float32 [768], P('fsdp')
- w_in_grad: float32 [768, 3072], P('fsdp')
- bias_in_grad: float32 [3072], P('fsdp')
- w_back_grad: float32 [3072, 768], P('fsdp')
- bias_back_grad: float32 [768], P('fsdp')
- ln2_gain_grad: float32 [768], P('fsdp')
- ln2_bias_grad: float32 [768], P('fsdp')
Inputs may be any that keep to these rules, and one draw needn't show every extreme that they name: `lengths`: every draw has a sequence that fills all 2048 slots. `pairing`: ctx index i stores storage blocks 2i and 2i + 1, which are the sequence's blocks t and 15 - t for some t; each block appears once.
All inputs are finite; a program needn't handle non-finite values.
Results may differ from a plain program's by a relative error of at most 0.02.
Values may be sent and summed in bfloat16 or wider, within the bound.
A program may use at most 192 MiB of HBM per device.

v0:
```python
import functools
import math

import jax
import jax.numpy as jnp
from jax import lax
from jax.experimental import pallas as pl
from jax.experimental.pallas import tpu as pltpu
from jax.sharding import PartitionSpec as P

HEADS = 12
HEAD_DIM = 64
NMEM = 10
BLK = 128


eps = 1e-12
neg_big = -1e30


def layer_norm(value, gain, shift):
    mean = jnp.mean(value, axis=-1, keepdims=True)
    centred = value - mean
    variance = jnp.mean(centred * centred, axis=-1, keepdims=True)
    return centred * lax.rsqrt(variance + eps) * gain + shift


def norm_back(value, gain, grad):
    mean = jnp.mean(value, axis=-1, keepdims=True)
    centred = value - mean
    scale = lax.rsqrt(jnp.mean(centred * centred, axis=-1, keepdims=True) + eps)
    unit = centred * scale
    scaled = grad * gain
    inner = (
        scaled
        - jnp.mean(scaled, axis=-1, keepdims=True)
        - unit * jnp.mean(scaled * unit, axis=-1, keepdims=True)
    )
    return (scale * inner, jnp.sum(grad * unit, axis=0), jnp.sum(grad, axis=0))


def block_width(count):
    return math.gcd(count, 512)


def places(pairing, start, count, half):
    rows = start + jnp.arange(count, dtype=jnp.int32)
    owners = rows // half
    spots = jnp.arange(pairing.shape[0], dtype=jnp.int32)
    picked = jnp.sum(jnp.where(owners[:, None] == spots[None, :], pairing[None, :], 0), axis=1)
    return picked * half + rows % half


def allowed_pairs(query_place, key_place, length):
    before = (key_place[None, :] <= query_place[:, None]) | (key_place[None, :] < NMEM)
    return (key_place[None, :] < length) & before


def heads_of(value):
    return value.reshape(value.shape[0], HEADS, HEAD_DIM)


def forward_fold(query_heads, query_place, pairing, length, half):

    def fold(carry, piece, start):
        keys, values = piece
        count = keys.shape[0]
        width = block_width(count)
        key_place = places(pairing, start, count, half)

        def step(index, state):
            top, total, summed = state
            offset = index * width
            key_heads = heads_of(lax.dynamic_slice_in_dim(keys, offset, width, 0))
            value_heads = heads_of(lax.dynamic_slice_in_dim(values, offset, width, 0))
            mask = allowed_pairs(
                query_place, lax.dynamic_slice_in_dim(key_place, offset, width, 0), length
            )[None]
            scores = (
                jnp.einsum(
                    "qhd,khd->hqk", query_heads, key_heads, preferred_element_type=jnp.float32
                )
                * 0.125
            )
            scores = jnp.where(mask, scores, neg_big)
            new_top = jnp.maximum(top, jnp.max(scores, axis=2))
            shrink = jnp.exp(top - new_top)
            probs = jnp.where(mask, jnp.exp(scores - new_top[:, :, None]), 0.0)
            total = total * shrink + jnp.sum(probs, axis=2)
            update = jnp.einsum(
                "hqk,khd->qhd",
                probs.astype(jnp.bfloat16),
                value_heads,
                preferred_element_type=jnp.float32,
            )
            summed = summed * jnp.transpose(shrink)[:, :, None] + update
            return (new_top, total, summed)

        return lax.fori_loop(0, count // width, step, carry)

    return fold


def query_grad_fold(query_heads, grad_heads, top_sum, delta, query_place, pairing, length, half):

    def fold(carry, piece, start):
        keys, values = piece
        count = keys.shape[0]
        width = block_width(count)
        key_place = places(pairing, start, count, half)

        def step(index, summed):
            offset = index * width
            key_heads = heads_of(lax.dynamic_slice_in_dim(keys, offset, width, 0))
            value_heads = heads_of(lax.dynamic_slice_in_dim(values, offset, width, 0))
            mask = allowed_pairs(
                query_place, lax.dynamic_slice_in_dim(key_place, offset, width, 0), length
            )[None]
            scores = (
                jnp.einsum(
                    "qhd,khd->hqk", query_heads, key_heads, preferred_element_type=jnp.float32
                )
                * 0.125
            )
            probs = jnp.where(mask, jnp.exp(scores - top_sum[:, :, None]), 0.0)
            prob_grad = jnp.einsum(
                "qhd,khd->hqk", grad_heads, value_heads, preferred_element_type=jnp.float32
            )
            score_grad = (probs * (prob_grad - delta[:, :, None])).astype(jnp.bfloat16)
            return (
                summed
                + jnp.einsum(
                    "hqk,khd->qhd", score_grad, key_heads, preferred_element_type=jnp.float32
                )
                * 0.125
            )

        return lax.fori_loop(0, count // width, step, carry)

    return fold


def key_terms(
    key_heads, value_heads, key_place, query_heads, grad_heads, top_sum, delta, query_place, length
):
    scores = (
        jnp.einsum("qhd,khd->hqk", query_heads, key_heads, preferred_element_type=jnp.float32)
        * 0.125
    )
    mask = allowed_pairs(query_place, key_place, length)[None]
    probs = jnp.where(mask, jnp.exp(scores - top_sum[:, :, None]), 0.0)
    prob_grad = jnp.einsum(
        "qhd,khd->hqk", grad_heads, value_heads, preferred_element_type=jnp.float32
    )
    score_grad = (probs * (prob_grad - delta[:, :, None])).astype(jnp.bfloat16)
    value_grad = jnp.einsum(
        "hqk,qhd->khd", probs.astype(jnp.bfloat16), grad_heads, preferred_element_type=jnp.float32
    )
    key_grad = (
        jnp.einsum("hqk,qhd->khd", score_grad, query_heads, preferred_element_type=jnp.float32)
        * 0.125
    )
    return (key_grad, value_grad)


def on_device_any(
    tokens,
    cotangent,
    lengths,
    pairing,
    w_qkv,
    bias_q,
    bias_v,
    w_out,
    bias_out,
    ln1_gain,
    ln1_bias,
    w_in,
    bias_in,
    w_back,
    bias_back,
    ln2_gain,
    ln2_bias,
):
    gathered = (
        lax.all_gather(w_qkv, "fsdp", axis=0, tiled=True),
        lax.all_gather(bias_q, "fsdp", axis=0, tiled=True),
        lax.all_gather(bias_v, "fsdp", axis=0, tiled=True),
        lax.all_gather(w_out, "fsdp", axis=0, tiled=True),
        lax.all_gather(bias_out, "fsdp", axis=0, tiled=True),
        lax.all_gather(ln1_gain, "fsdp", axis=0, tiled=True),
        lax.all_gather(ln1_bias, "fsdp", axis=0, tiled=True),
        lax.all_gather(w_in, "fsdp", axis=0, tiled=True),
        lax.all_gather(bias_in, "fsdp", axis=0, tiled=True),
        lax.all_gather(w_back, "fsdp", axis=0, tiled=True),
        lax.all_gather(bias_back, "fsdp", axis=0, tiled=True),
        lax.all_gather(ln2_gain, "fsdp", axis=0, tiled=True),
        lax.all_gather(ln2_bias, "fsdp", axis=0, tiled=True),
    )
    (
        qkv_all,
        query_bias,
        value_bias,
        out_all,
        out_bias,
        gain_one,
        shift_one,
        in_all,
        in_bias,
        back_all,
        back_bias,
        gain_two,
        shift_two,
    ) = gathered
    rows = tokens.shape[1]
    half = rows // 2
    width = tokens.shape[2]
    length = lengths[0]
    query_place = places(pairing, lax.axis_index("ctx") * rows, rows, half)
    valid = query_place < length
    inputs = tokens[0]
    proj = jnp.dot(inputs, qkv_all, preferred_element_type=jnp.float32)
    queries = (proj[:, :width] + query_bias.astype(jnp.float32)).astype(jnp.bfloat16)
    keys = proj[:, width : 2 * width].astype(jnp.bfloat16)
    values = (proj[:, 2 * width :] + value_bias.astype(jnp.float32)).astype(jnp.bfloat16)
    query_heads = heads_of(queries)
    start_state = (
        jnp.full((HEADS, rows), neg_big, jnp.float32),
        jnp.zeros((HEADS, rows), jnp.float32),
        jnp.zeros((rows, HEADS, HEAD_DIM), jnp.float32),
    )
    fold = forward_fold(query_heads, query_place, pairing, length, half)
    top, total, summed = fold(
        start_state,
        (
            lax.all_gather(keys, "ctx", axis=0, tiled=True),
            lax.all_gather(values, "ctx", axis=0, tiled=True),
        ),
        jnp.int32(0),
    )
    top_sum = top + jnp.log(total)
    attended = (summed / jnp.transpose(total)[:, :, None]).reshape(rows, width)
    attended_low = attended.astype(jnp.bfloat16)
    resid_one = (
        inputs.astype(jnp.float32)
        + jnp.dot(attended_low, out_all, preferred_element_type=jnp.float32)
        + out_bias.astype(jnp.float32)
    )
    hidden = layer_norm(resid_one, gain_one.astype(jnp.float32), shift_one.astype(jnp.float32))
    hidden_low = hidden.astype(jnp.bfloat16)
    upper = jnp.dot(hidden_low, in_all, preferred_element_type=jnp.float32) + in_bias.astype(
        jnp.float32
    )
    active, gelu_back = jax.vjp(lambda value: jax.nn.gelu(value, approximate=False), upper)
    active_low = active.astype(jnp.bfloat16)
    resid_two = (
        hidden
        + jnp.dot(active_low, back_all, preferred_element_type=jnp.float32)
        + back_bias.astype(jnp.float32)
    )
    normed = layer_norm(resid_two, gain_two.astype(jnp.float32), shift_two.astype(jnp.float32))
    output = jnp.where(valid[:, None], normed, 0.0)
    qkv_back, out_back, gain_one_back, in_back, back_back, gain_two_back = (
        qkv_all,
        out_all,
        gain_one,
        in_all,
        back_all,
        gain_two,
    )
    grad_y = jnp.where(valid[:, None], cotangent[0].astype(jnp.float32), 0.0)
    grad_resid_two, gain_two_grad, shift_two_grad = norm_back(
        resid_two, gain_two_back.astype(jnp.float32), grad_y
    )
    grad_mixed = grad_resid_two.astype(jnp.bfloat16)
    back_grad = jnp.einsum("tf,td->fd", active_low, grad_mixed, preferred_element_type=jnp.float32)
    back_bias_grad = jnp.sum(grad_mixed.astype(jnp.float32), axis=0)
    grad_active = jnp.einsum("td,fd->tf", grad_mixed, back_back, preferred_element_type=jnp.float32)
    (grad_upper,) = gelu_back(grad_active)
    grad_upper_low = grad_upper.astype(jnp.bfloat16)
    in_grad = jnp.einsum(
        "td,tf->df", hidden_low, grad_upper_low, preferred_element_type=jnp.float32
    )
    in_bias_grad = jnp.sum(grad_upper_low.astype(jnp.float32), axis=0)
    grad_hidden = grad_resid_two + jnp.einsum(
        "tf,df->td", grad_upper_low, in_back, preferred_element_type=jnp.float32
    )
    grad_resid_one, gain_one_grad, shift_one_grad = norm_back(
        resid_one, gain_one_back.astype(jnp.float32), grad_hidden
    )
    grad_branch = grad_resid_one.astype(jnp.bfloat16)
    out_grad = jnp.einsum(
        "tc,td->cd", attended_low, grad_branch, preferred_element_type=jnp.float32
    )
    out_bias_grad = jnp.sum(grad_branch.astype(jnp.float32), axis=0)
    grad_attended = jnp.einsum(
        "td,cd->tc", grad_branch, out_back, preferred_element_type=jnp.float32
    ).astype(jnp.bfloat16)
    grad_heads = heads_of(grad_attended)
    delta = jnp.transpose(jnp.sum(grad_heads.astype(jnp.float32) * heads_of(attended), axis=2))
    query_fold = query_grad_fold(
        query_heads, grad_heads, top_sum, delta, query_place, pairing, length, half
    )
    empty_heads = jnp.zeros((rows, HEADS, HEAD_DIM), jnp.float32)
    query_grad = query_fold(
        empty_heads,
        (
            lax.all_gather(keys, "ctx", axis=0, tiled=True),
            lax.all_gather(values, "ctx", axis=0, tiled=True),
        ),
        jnp.int32(0),
    )
    stats = jnp.concatenate([jnp.transpose(top_sum), jnp.transpose(delta)], axis=1)
    stats_all = lax.all_gather(stats, "ctx", axis=0, tiled=True)
    key_heads = heads_of(keys)
    value_heads = heads_of(values)
    query_in = lax.all_gather(queries, "ctx", axis=0, tiled=True)
    grad_in = lax.all_gather(grad_attended, "ctx", axis=0, tiled=True)
    count = query_in.shape[0]
    span = block_width(count)
    place_in = places(pairing, jnp.int32(0), count, half)

    def step(index, state):
        offset = index * span
        query_block = heads_of(lax.dynamic_slice_in_dim(query_in, offset, span, 0))
        grad_block = heads_of(lax.dynamic_slice_in_dim(grad_in, offset, span, 0))
        stats_block = lax.dynamic_slice_in_dim(stats_all, offset, span, 0)
        place_block = lax.dynamic_slice_in_dim(place_in, offset, span, 0)
        key_part, value_part = key_terms(
            key_heads,
            value_heads,
            query_place,
            query_block,
            grad_block,
            jnp.transpose(stats_block[:, :HEADS]),
            jnp.transpose(stats_block[:, HEADS:]),
            place_block,
            length,
        )
        return (state[0] + key_part, state[1] + value_part)

    key_sum, value_sum = lax.fori_loop(0, count // span, step, (empty_heads, empty_heads))
    key_grad = key_sum.reshape(rows, width)
    value_grad = value_sum.reshape(rows, width)
    grad_proj = jnp.concatenate(
        [
            query_grad.reshape(rows, width).astype(jnp.bfloat16),
            key_grad.astype(jnp.bfloat16),
            value_grad.astype(jnp.bfloat16),
        ],
        axis=1,
    )
    qkv_grad = jnp.einsum("td,tf->df", inputs, grad_proj, preferred_element_type=jnp.float32)
    query_bias_grad = jnp.sum(grad_proj[:, :width].astype(jnp.float32), axis=0)
    value_bias_grad = jnp.sum(grad_proj[:, 2 * width :].astype(jnp.float32), axis=0)
    token_grad = grad_resid_one + jnp.einsum(
        "tf,df->td", grad_proj, qkv_back, preferred_element_type=jnp.float32
    )
    grads = (
        qkv_grad,
        query_bias_grad,
        value_bias_grad,
        out_grad,
        out_bias_grad,
        gain_one_grad,
        shift_one_grad,
        in_grad,
        in_bias_grad,
        back_grad,
        back_bias_grad,
        gain_two_grad,
        shift_two_grad,
    )
    shards = (
        lax.psum_scatter(
            grads[0].astype(jnp.bfloat16), "fsdp", scatter_dimension=0, tiled=True
        ).astype(jnp.float32),
        lax.psum_scatter(
            grads[1].astype(jnp.bfloat16), "fsdp", scatter_dimension=0, tiled=True
        ).astype(jnp.float32),
        lax.psum_scatter(
            grads[2].astype(jnp.bfloat16), "fsdp", scatter_dimension=0, tiled=True
        ).astype(jnp.float32),
        lax.psum_scatter(
            grads[3].astype(jnp.bfloat16), "fsdp", scatter_dimension=0, tiled=True
        ).astype(jnp.float32),
        lax.psum_scatter(
            grads[4].astype(jnp.bfloat16), "fsdp", scatter_dimension=0, tiled=True
        ).astype(jnp.float32),
        lax.psum_scatter(
            grads[5].astype(jnp.bfloat16), "fsdp", scatter_dimension=0, tiled=True
        ).astype(jnp.float32),
        lax.psum_scatter(
            grads[6].astype(jnp.bfloat16), "fsdp", scatter_dimension=0, tiled=True
        ).astype(jnp.float32),
        lax.psum_scatter(
            grads[7].astype(jnp.bfloat16), "fsdp", scatter_dimension=0, tiled=True
        ).astype(jnp.float32),
        lax.psum_scatter(
            grads[8].astype(jnp.bfloat16), "fsdp", scatter_dimension=0, tiled=True
        ).astype(jnp.float32),
        lax.psum_scatter(
            grads[9].astype(jnp.bfloat16), "fsdp", scatter_dimension=0, tiled=True
        ).astype(jnp.float32),
        lax.psum_scatter(
            grads[10].astype(jnp.bfloat16), "fsdp", scatter_dimension=0, tiled=True
        ).astype(jnp.float32),
        lax.psum_scatter(
            grads[11].astype(jnp.bfloat16), "fsdp", scatter_dimension=0, tiled=True
        ).astype(jnp.float32),
        lax.psum_scatter(
            grads[12].astype(jnp.bfloat16), "fsdp", scatter_dimension=0, tiled=True
        ).astype(jnp.float32),
    )
    totals = (
        lax.psum(shards[0].astype(jnp.bfloat16), "ctx").astype(jnp.float32),
        lax.psum(shards[1].astype(jnp.bfloat16), "ctx").astype(jnp.float32),
        lax.psum(shards[2].astype(jnp.bfloat16), "ctx").astype(jnp.float32),
        lax.psum(shards[3].astype(jnp.bfloat16), "ctx").astype(jnp.float32),
        lax.psum(shards[4].astype(jnp.bfloat16), "ctx").astype(jnp.float32),
        lax.psum(shards[5].astype(jnp.bfloat16), "ctx").astype(jnp.float32),
        lax.psum(shards[6].astype(jnp.bfloat16), "ctx").astype(jnp.float32),
        lax.psum(shards[7].astype(jnp.bfloat16), "ctx").astype(jnp.float32),
        lax.psum(shards[8].astype(jnp.bfloat16), "ctx").astype(jnp.float32),
        lax.psum(shards[9].astype(jnp.bfloat16), "ctx").astype(jnp.float32),
        lax.psum(shards[10].astype(jnp.bfloat16), "ctx").astype(jnp.float32),
        lax.psum(shards[11].astype(jnp.bfloat16), "ctx").astype(jnp.float32),
        lax.psum(shards[12].astype(jnp.bfloat16), "ctx").astype(jnp.float32),
    )
    return (output[None], token_grad[None]) + tuple(totals)


def low_lanes(shape):
    return lax.broadcasted_iota(jnp.int32, shape, 1) < 64


def spot_of(pair_ref, place):
    found = jnp.int32(0)
    for s in range(pair_ref.shape[0]):
        found = jnp.where(pair_ref[s] == place, s, found)
    return found


def attend(c, length, spot, keep_ref, mix_ref, lse_ref, turned_ref):
    left = low_lanes((256, BLK))
    zero = jnp.zeros((), jnp.bfloat16)
    keys = 256 * (c + 1)
    own = keep_ref[0, 2 * c : 2 * c + 2].reshape(256, BLK)
    shared = keep_ref[0, 2 * c + spot]
    query = jnp.concatenate(
        [jnp.where(left, own, zero), jnp.where(left[:BLK], zero, shared)], axis=0
    ) * jnp.bfloat16(0.125)
    key = keep_ref[1, : 2 * c + 2].reshape(keys, BLK)
    value = keep_ref[2, : 2 * c + 2].reshape(keys, BLK)
    scores = mask_scores(dot_nt(key, query), c, spot, length, 0, True)
    top = jnp.max(scores, axis=0, keepdims=True)
    probs = jnp.exp(scores - top)
    total = jnp.sum(probs, axis=0, keepdims=True)
    summed = lax.dot_general(
        value, probs.astype(jnp.bfloat16), (((0,), (0,)), ((), ())),
        preferred_element_type=jnp.float32,
    ) / total
    lse_ref[c] = top + jnp.log(total)
    part = summed[64:, 256:]
    none = jnp.zeros_like(part)
    first = jnp.where(spot == 0, part, none)
    second = jnp.where(spot == 0, none, part)
    mixed = jnp.concatenate([summed[:64, :256], jnp.concatenate([first, second], axis=1)], axis=0)
    mix_ref[c] = mixed
    turned_ref[2 * c : 2 * c + 2] = (
        jnp.transpose(mixed).astype(jnp.bfloat16).reshape(2, BLK, BLK)
    )


def mask_scores(scores, c, spot, length, start, edged):
    keys, width = scores.shape
    row = start + lax.broadcasted_iota(jnp.int32, (keys, width), 0)
    scores = jnp.where(row < length, scores, neg_big)
    if not edged:
        return scores
    edge = 256 * c
    lane = lax.broadcasted_iota(jnp.int32, (256, width), 1)
    query_place = edge + jnp.where(lane < 256, lane, lane - 256 + spot * BLK)
    key_place = edge + lax.broadcasted_iota(jnp.int32, (256, width), 0)
    seen = key_place <= query_place
    if c == 0:
        seen = seen | (key_place < NMEM)
    tail = jnp.where(seen, scores[keys - 256 :], neg_big)
    if keys == 256:
        return tail
    return jnp.concatenate([scores[: keys - 256], tail], axis=0)


def attend_back(
    c, length, spot, keep_ref, g_ref, mix_ref, lse_ref, q_sum, k_sum, v_sum
):
    zero = jnp.zeros((), jnp.bfloat16)
    left = low_lanes((256, BLK))
    left_half = left[:BLK]
    own = keep_ref[0, 2 * c : 2 * c + 2].reshape(256, BLK)
    shared = keep_ref[0, 2 * c + spot]
    query = jnp.concatenate(
        [jnp.where(left, own, zero), jnp.where(left_half, zero, shared)], axis=0
    ) * jnp.bfloat16(0.125)
    g_own = g_ref[2 * c : 2 * c + 2].reshape(256, BLK)
    g_shared = g_ref[2 * c + spot]
    grad = jnp.concatenate(
        [jnp.where(left, g_own, zero), jnp.where(left_half, zero, g_shared)], axis=0
    )
    turned = jnp.transpose(g_own.astype(jnp.float32)) * mix_ref[c]
    delta_own = jnp.sum(turned[:64], axis=0, keepdims=True)
    delta_pair = jnp.sum(turned[64:], axis=0, keepdims=True)
    delta = jnp.concatenate(
        [delta_own, jnp.where(spot == 0, delta_pair[:, :BLK], delta_pair[:, BLK:])], axis=1
    )
    lse = lse_ref[c]
    q_grad = jnp.zeros((384, BLK), jnp.float32)
    last = 2 * c + 2
    step = 8
    for low_block in range(0, last, step):
        high_block = min(low_block + step, last)
        cut = slice(low_block, high_block)
        count = high_block - low_block
        key = keep_ref[1, cut].reshape(count * BLK, BLK)
        value = keep_ref[2, cut].reshape(count * BLK, BLK)
        scores = mask_scores(
            dot_nt(key, query), c, spot, length, low_block * BLK, high_block == last
        )
        probs = jnp.exp(scores - lse)
        score_grad = (probs * (dot_nt(value, grad) - delta)).astype(jnp.bfloat16)
        v_part = dot_nn(probs.astype(jnp.bfloat16), grad)
        k_part = dot_nn(score_grad, query)
        v_sum[cut] += v_part.reshape(count, BLK, BLK)
        k_sum[cut] += k_part.reshape(count, BLK, BLK)
        q_grad = q_grad + lax.dot_general(
            score_grad, key, (((0,), (0,)), ((), ())), preferred_element_type=jnp.float32
        )
    q_grad = q_grad * 0.125
    part = q_grad[256:]
    none = jnp.zeros_like(part)
    first = jnp.where(spot == 0, part, none)
    second = jnp.where(spot == 0, none, part)
    q_sum[2 * c : 2 * c + 2] = jnp.where(
        left, q_grad[:256], jnp.concatenate([first, second], axis=0)
    ).reshape(2, BLK, BLK)


def smem():
    return pl.BlockSpec(memory_space=pltpu.SMEM)


def vmem():
    return pl.BlockSpec(memory_space=pltpu.VMEM)


MESH = pl.DeviceIdType.MESH


def remote(src, dst, sems, at, peer):
    return pltpu.make_async_remote_copy(
        src_ref=src, dst_ref=dst, send_sem=sems.at[(0,) + at], recv_sem=sems.at[(1,) + at],
        device_id=peer, device_id_type=MESH,
    )


def greet(peers):
    barrier = pltpu.get_barrier_semaphore()
    for peer in peers:
        pl.semaphore_signal(barrier, inc=1, device_id=peer, device_id_type=MESH)
    pl.semaphore_wait(barrier, len(peers))


def ring_peers(n):
    me = lax.axis_index("ctx")
    return [{"ctx": lax.rem(me + k, n)} for k in range(1, n)]


def two(block):
    return pl.ds(2 * block, 2)


def one(block):
    return block


def exchange_copies(n, in_ref, out_ref, sems, at=two):
    me = lax.axis_index("ctx")
    copies = []
    for k in range(1, n):
        peer = lax.rem(me + k, n)
        copies.append(
            remote(in_ref.at[at(peer)], out_ref.at[at(me)], sems, (k,), {"ctx": peer})
        )
    return copies


def own_copy(in_ref, out_ref, sem, at=two):
    me = lax.axis_index("ctx")
    return pltpu.make_async_copy(in_ref.at[at(me)], out_ref.at[at(me)], sem)


def beside(first, second, axis):
    return jnp.concatenate([first, second], axis=axis)


def fold(first, second, shared):
    return beside(
        beside(first[:, :HEAD_DIM], second[:, :HEAD_DIM], 1),
        beside(shared[:HEAD_DIM], shared[HEAD_DIM:], 1),
        0,
    )


def fold_pair(value, spot, lead):
    first, second = value[:BLK], value[BLK:]
    return fold(
        first, second, jnp.where(lead == spot, first[:, HEAD_DIM:], second[:, HEAD_DIM:])
    )


def unfold_shared(message):
    return beside(message[BLK:, :HEAD_DIM], message[BLK:, HEAD_DIM:], 0)


def unfold_block(message, later):
    own = jnp.where(later == 0, message[:BLK, :HEAD_DIM], message[:BLK, HEAD_DIM:])
    return beside(own, unfold_shared(message), 1)


def join_folded(messages, lead):
    pieces = []
    for group in range(HEADS // 3):
        pair = [messages(2 * group), messages(2 * group + 1)]
        for message in pair:
            pieces.append(beside(message[:BLK, :HEAD_DIM], message[:BLK, HEAD_DIM:], 0))
        even, odd = [unfold_shared(message) for message in pair]
        pieces.append(
            beside(jnp.where(lead == 0, even, odd), jnp.where(lead == 0, odd, even), 0)
        )
    return jnp.concatenate(pieces, axis=1)


def both(ref, peer):
    value = ref[2 * peer : 2 * peer + 2]
    return value.reshape(-1, value.shape[2])


def join_pairs(pairs):
    pieces = []
    for group in range(HEADS // 3):
        first, second = pairs(2 * group), pairs(2 * group + 1)
        shared = first[:, HEAD_DIM:].astype(jnp.float32) + second[:, HEAD_DIM:].astype(jnp.float32)
        pieces += [first[:, :HEAD_DIM], second[:, :HEAD_DIM], shared.astype(jnp.bfloat16)]
    return jnp.concatenate(pieces, axis=1)


def pair_of(value, peer):
    own = 3 * (peer // 2) + peer % 2
    shared = 3 * (peer // 2) + 2
    cut = lambda head: value[:, head * HEAD_DIM : (head + 1) * HEAD_DIM]
    return jnp.concatenate([cut(own), cut(shared)], axis=1)


def dot_nn(a, b):
    return jnp.dot(a, b, preferred_element_type=jnp.float32)


def dot_nt(a, b):
    return lax.dot_general(a, b, (((1,), (1,)), ((), ())), preferred_element_type=jnp.float32)


def column_sum(value):
    return jnp.sum(value, axis=0, keepdims=True)


def unit_of(value):
    mean = jnp.mean(value, axis=-1, keepdims=True)
    centred = value - mean
    scale = lax.rsqrt(jnp.mean(centred * centred, axis=-1, keepdims=True) + eps)
    return centred * scale, scale


def unit_back(unit, scale, scaled):
    return scale * (
        scaled
        - jnp.mean(scaled, axis=-1, keepdims=True)
        - unit * jnp.mean(scaled * unit, axis=-1, keepdims=True)
    )


(ROW_BQ, ROW_BV, ROW_BO, ROW_G1, ROW_S1, ROW_BB, ROW_G2, ROW_S2, ROW_BI) = range(9)


def gather_copies(src, full, sems, index):
    fsdp = lax.axis_index("fsdp")
    x, core = fsdp // 2, lax.rem(fsdp, 2)
    sibling, across = {"fsdp": 2 * x + 1 - core}, {"fsdp": 2 * (1 - x) + core}
    other = 2 * (1 - x) + core
    return (
        remote(src, full.at[fsdp], sems, (index, 0), across),
        remote(src, full.at[fsdp], sems, (index, 1), sibling),
        remote(full.at[other], full.at[other], sems, (index, 2), sibling),
    )


def chip_peers():
    fsdp = lax.axis_index("fsdp")
    x, core = fsdp // 2, lax.rem(fsdp, 2)
    return [{"fsdp": 2 * x + 1 - core}, {"fsdp": 2 * (1 - x) + core}]


def split_gather(src, full, sems, parts):
    ctx, fsdp = lax.axis_index("ctx"), lax.axis_index("fsdp")
    z, y = ctx // 2, lax.rem(ctx, 2)
    x, core = fsdp // 2, lax.rem(fsdp, 2)
    sibling, across = {"fsdp": 2 * x + 1 - core}, {"fsdp": 2 * (1 - x) + core}
    over_y = {"ctx": 2 * z + 1 - y}
    other = 2 * (1 - x) + core
    count = src.shape[0] // 2
    here = pl.ds(pl.multiple_of(y * count, count), count)
    there = pl.ds(pl.multiple_of((1 - y) * count, count), count)
    cross, side, on, off, whole = [], [], [], [], []
    for p in range(parts):
        width = src.shape[1] // parts
        cols = slice(p * width, (p + 1) * width)
        moved = full.at[other, here, cols]
        late = full.at[other, there, cols]
        cross.append(remote(src.at[here, cols], full.at[fsdp, here, cols], sems, (0, p), across))
        side.append(remote(moved, moved, sems, (1, p), over_y))
        on.append(remote(moved, moved, sems, (2, p), sibling))
        off.append(remote(late, late, sems, (3, p), sibling))
        whole.append(remote(src.at[:, cols], full.at[fsdp, :, cols], sems, (4, p), sibling))
    return cross, side, on, off, whole


def passed(split, p):
    cross, side, on, off, whole = split
    cross[p].wait_recv()
    side[p].start()
    on[p].start()


def handed(split, p):
    cross, side, on, off, whole = split
    side[p].wait_recv()
    off[p].start()


def gathered(split, p):
    cross, side, on, off, whole = split
    for copies in (whole, on, off):
        copies[p].wait_recv()


def front_kernel(
    n, pair_ref, len_ref, *refs
):
    vectors, refs = refs[:9], refs[9:]
    (
        tokens_ref, cot_ref, qkv_src, out_src, in_src, back_src,
        output_ref, grad_ref, left_ref, right_ref, resid_ref, sums_ref,
        keep_ref, mix_ref, lse_ref, qkv_ref,
        small_out, small, rows_ref, token_buf, cot, w_qkv, w_out, w_in, w_back, send_folded, send,
        packed_q, packed_k, packed_v, keep, mix,
        lse, turned, mixed_out, mixed_in, active, slope, output, grad_out, left, right, resid, sums,
        small_sem, qkv_sem, in_split_sem, back_split_sem, gather_sem, send_q, send_k, send_v, in_sem, own_sem, load_sem, ship_sem,
    ) = refs
    send_sem = (send_q, send_k, send_v)
    packed = (packed_q, packed_k, packed_v)
    low, wide = jnp.bfloat16, jnp.float32
    ctx, fsdp = lax.axis_index("ctx"), lax.axis_index("fsdp")
    x, core = fsdp // 2, lax.rem(fsdp, 2)
    spot = lax.rem(ctx, 2)
    lead = lax.rem(pair_ref[2 * ctx], 2)
    width = token_buf.shape[1]
    count = in_src.shape[1] // width
    loads = [
        pltpu.make_async_copy(src, dst, load_sem.at[i])
        for i, (src, dst) in enumerate(
            [
                (tokens_ref, token_buf),
                (cot_ref, cot),
                (qkv_src, w_qkv.at[fsdp]),
                (out_src, w_out.at[fsdp]),
                (in_src, w_in.at[fsdp]),
                (back_src, w_back.at[fsdp]),
            ]
        )
    ]
    cot_load = loads[1]
    for cp in loads[:3]:
        cp.start()
    part = width // 4
    small_out[...] = jnp.zeros_like(small_out)
    for i in range(8):
        small_out[i : i + 1] = vectors[i][...].astype(wide).reshape(1, part)
    inner_bias = vectors[8][...].astype(wide).reshape(1, -1)
    for j in range(4):
        small_out[8 + j : 9 + j] = inner_bias[:, j * part : (j + 1) * part]
    greet(ring_peers(n) + chip_peers())
    smalls = gather_copies(small_out, small, small_sem, 0)
    qkv_split = split_gather(qkv_src, w_qkv, qkv_sem, 3)
    in_split = split_gather(in_src, w_in, in_split_sem, count)
    back_split = split_gather(back_src, w_back, back_split_sem, 2)
    splits = (qkv_split, in_split, back_split)
    for step in (0, 1):
        smalls[step].start()
    for cp in qkv_split[0] + qkv_split[4]:
        cp.start()
    for cp in loads[3:]:
        cp.start()
    shards = gather_copies(out_src, w_out, gather_sem, 0)
    small[fsdp] = small_out[...]
    smalls[0].wait_recv()
    smalls[2].start()
    passed(qkv_split, 0)
    loads[0].wait()
    tokens = token_buf[...]
    left[0] = jnp.transpose(tokens).reshape(4, -1, 2 * BLK)
    smalls[1].wait_recv()
    smalls[2].wait_recv()
    for f in range(4):
        cols = slice(f * part, (f + 1) * part)
        rows_ref[:8, cols] = small[f, :8]
        for j in range(4):
            rows_ref[ROW_BI + f : ROW_BI + f + 1, j * part : (j + 1) * part] = small[
                f, 8 + j : 9 + j
            ]
    rows_ref[12:] = jnp.zeros_like(rows_ref[12:])
    row = lambda i: rows_ref[i : i + 1, :]
    passed(qkv_split, 1)
    handed(qkv_split, 0)
    passed(qkv_split, 2)
    for cp in shards[:2]:
        cp.start()
    for split in (in_split, back_split):
        for cp in split[0] + split[4]:
            cp.start()
    loads[2].wait()
    sends = []
    for p, bias in enumerate((ROW_BQ, None, ROW_BV)):
        if p:
            handed(qkv_split, p)
        gathered(qkv_split, p)
        value = dot_nn(tokens, w_qkv[:, :, p * width : (p + 1) * width].reshape(width, width))
        if bias is not None:
            value = value + row(bias)
        value = value.astype(low)
        for peer in range(n):
            both_heads = pair_of(value, peer)
            if p:
                send[p - 1, 2 * peer : 2 * peer + 2] = both_heads.reshape(2, BLK, BLK)
            else:
                send_folded[peer] = fold_pair(both_heads, peer % 2, lead)
        source, at = (send.at[p - 1], two) if p else (send_folded, one)
        copies = exchange_copies(n, source, packed[p], send_sem[p], at)
        copies.append(own_copy(source, packed[p], own_sem.at[2 + p], at))
        for cp in copies:
            cp.start()
        sends.append(copies)
    shipped = []

    def ship(src, dst):
        cp = pltpu.make_async_copy(src, dst, ship_sem.at[len(shipped)])
        cp.start()
        shipped.append(cp)

    ship(w_qkv, qkv_ref)
    spots = lax.broadcasted_iota(jnp.int32, (2 * BLK, 1), 0)
    place = jnp.where(
        spots < BLK,
        pair_ref[2 * ctx] * BLK + spots,
        pair_ref[2 * ctx + 1] * BLK + spots - BLK,
    )
    valid = place < len_ref[0]
    shards[0].wait_recv()
    shards[2].start()
    for p in range(count):
        passed(in_split, p)
        if p:
            handed(in_split, p - 1)
    passed(back_split, 0)
    handed(in_split, count - 1)
    spots_of = [spot_of(pair_ref, b) for b in range(2 * n)]
    for p in range(3):
        sends[p][-1].wait()
        for cp in sends[p][:-1]:
            cp.wait_recv()
        for b in range(2 * n):
            if p:
                keep[p, b] = packed[p][spots_of[b]]
            else:
                keep[p, b] = unfold_block(
                    packed[p][lax.div(spots_of[b], 2)], lax.rem(spots_of[b], 2)
                )
    passed(back_split, 1)

    ship(keep, keep_ref)
    for c in range(n):
        attend(c, len_ref[0], spot, keep, mix, lse, turned)
    for peer in range(n):
        first, second = turned[pair_ref[2 * peer]], turned[pair_ref[2 * peer + 1]]
        mixed_out[peer] = fold(first, second, first[:, HEAD_DIM:] + second[:, HEAD_DIM:])
    copies = exchange_copies(n, mixed_out, mixed_in, in_sem, one)
    for cp in copies:
        cp.start()
    own_mixed = own_copy(mixed_out, mixed_in, own_sem.at[1], one)
    own_mixed.start()
    ship(mix, mix_ref)
    ship(lse, lse_ref)
    sums[...] = jnp.zeros_like(sums)
    for cp in loads[3:]:
        cp.wait()
    for p in range(2):
        handed(back_split, p)
    shards[1].wait_recv()
    shards[2].wait_recv()
    for p in range(count):
        gathered(in_split, p)
    own_mixed.wait()
    for cp in copies:
        cp.wait_recv()
    attended = join_folded(lambda peer: mixed_in[peer], lead)
    resid_one = (
        tokens.astype(wide)
        + dot_nn(attended, w_out[...].reshape(width, width))
        + row(ROW_BO)
    )
    unit_one, scale_one = unit_of(resid_one)
    hidden = unit_one * row(ROW_G1) + row(ROW_S1)
    hidden_low = hidden.astype(low)
    resid_two = hidden + row(ROW_BB)
    cut = lambda t: pl.ds(pl.multiple_of(t * width, width), width)
    order = [fsdp, 2 * x + 1 - core, 2 * (1 - x) + core, 2 * (1 - x) + 1 - core]
    for step, t in enumerate(order):
        bias = rows_ref[pl.ds(ROW_BI + t, 1), :]
        upper = dot_nn(hidden_low, w_in[:, :, cut(t)].reshape(width, width)) + bias
        share = 0.5 * (1.0 + lax.erf(upper * (0.5**0.5)))
        slope[t] = share + upper * (jnp.exp(-0.5 * upper * upper) * (2 * math.pi) ** -0.5)
        some = (upper * share).astype(low)
        active[t] = some
        if step == 0:
            gathered(back_split, 0)
            gathered(back_split, 1)
        resid_two = resid_two + dot_nn(some, w_back[t])
    unit_two, scale_two = unit_of(resid_two)
    output[...] = jnp.where(valid, unit_two * row(ROW_G2) + row(ROW_S2), 0.0)
    cot_load.wait()
    grad_y = jnp.where(valid, cot[...].astype(wide), 0.0)
    sums[ROW_G2 : ROW_G2 + 1, :] = column_sum(grad_y * unit_two)
    sums[ROW_S2 : ROW_S2 + 1, :] = column_sum(grad_y)
    grad_resid_two = unit_back(unit_two, scale_two, grad_y * row(ROW_G2))
    grad_mixed = grad_resid_two.astype(low)
    right[5] = grad_mixed
    sums[ROW_BB : ROW_BB + 1, :] = column_sum(grad_mixed.astype(wide))
    ship(output, output_ref)
    left[1] = jnp.transpose(attended).reshape(4, -1, 2 * BLK)
    left[2] = jnp.transpose(hidden_low).reshape(4, -1, 2 * BLK)
    for f in range(4):
        turned = jnp.transpose(active[f])
        for r in range(4):
            left[3 + r, f] = turned[r * width // 4 : (r + 1) * width // 4]
    ship(left, left_ref)
    grad_hidden = grad_resid_two
    for t in range(count):
        grad_upper = (dot_nt(grad_mixed, w_back[t]) * slope[t]).astype(low)
        right[1 + t] = grad_upper
        sums[ROW_BI + t : ROW_BI + t + 1, :] = column_sum(grad_upper.astype(wide))
        grad_hidden = grad_hidden + dot_nt(grad_upper, w_in[:, :, cut(t)].reshape(width, width))
    sums[ROW_G1 : ROW_G1 + 1, :] = column_sum(grad_hidden * unit_one)
    sums[ROW_S1 : ROW_S1 + 1, :] = column_sum(grad_hidden)
    grad_resid_one = unit_back(unit_one, scale_one, grad_hidden * row(ROW_G1))
    resid[...] = grad_resid_one
    grad_branch = grad_resid_one.astype(low)
    right[0] = grad_branch
    sums[ROW_BO : ROW_BO + 1, :] = column_sum(grad_branch.astype(wide))
    ship(resid, resid_ref)
    ship(right, right_ref)
    ship(sums, sums_ref)
    grad_attended = dot_nt(grad_branch, w_out[...].reshape(width, width)).astype(low)
    for peer in range(n):
        grad_out[peer] = fold_pair(pair_of(grad_attended, peer), peer % 2, lead)
    ship(grad_out, grad_ref)
    for cps in (smalls, shards, copies) + sum(splits, ()):
        for cp in cps:
            cp.wait_send()
    for cps in sends:
        for cp in cps[:-1]:
            cp.wait_send()
    for cp in shipped:
        cp.wait()


def front(pairing, lengths, vectors, tokens, cotangent, w_qkv, w_out, w_in, w_back, n, name):
    count, width = tokens.shape
    low, wide = jnp.bfloat16, jnp.float32
    dma = pltpu.SemaphoreType.DMA
    shape = jax.ShapeDtypeStruct
    hbm = pl.BlockSpec(memory_space=pltpu.HBM)
    vec = pltpu.VMEM((16, width // 4), wide)
    results = [
        ((count, width), wide),
        ((n, BLK + HEAD_DIM, BLK), low),
        ((7, 4, width // 4, count), low),
        ((6, count, width), low),
        ((count, width), wide),
        ((16, width), wide),
        ((3, 2 * n, BLK, BLK), low),
        ((n, BLK, 2 * BLK), wide),
        ((n, 1, 3 * BLK), wide),
        ((4,) + w_qkv.shape, low),
    ]
    output, grad, left, right, resid, sums, keep, mix, lse, qkv = [pltpu.VMEM(*r) for r in results]
    blocks = pltpu.VMEM((2 * n, BLK, BLK), low)
    return pl.pallas_call(
        functools.partial(front_kernel, n),
        out_shape=tuple(shape(*r) for r in results),
        in_specs=[smem(), smem()] + [vmem()] * 9 + [hbm] * 6,
        out_specs=(hbm,) * 10,
        scratch_shapes=[
            vec,
            pltpu.VMEM((4, 16, width // 4), wide),
            pltpu.VMEM((16, width), wide),
            pltpu.VMEM((count, width), low),
            pltpu.VMEM((count, width), low),
            qkv,
            pltpu.VMEM((4,) + w_out.shape, low),
            pltpu.VMEM((4,) + w_in.shape, low),
            pltpu.VMEM((4,) + w_back.shape, low),
            grad,
            pltpu.VMEM((2, 2 * n, BLK, BLK), low),
            grad,
            blocks,
            blocks,
            keep,
            mix,
            lse,
            blocks,
            grad,
            grad,
            pltpu.VMEM((4, count, width), low),
            pltpu.VMEM((4, count, width), wide),
            output,
            grad,
            left,
            right,
            resid,
            sums,
            dma((2, 1, 3)),
            dma((2, 5, 3)),
            dma((2, 5, 4)),
            dma((2, 5, 2)),
            dma((2, 1, 3)),
            dma((2, n)),
            dma((2, n)),
            dma((2, n)),
            dma((2, n)),
            dma((5,)),
            dma((6,)),
            dma((10,)),
        ],
        compiler_params=pltpu.CompilerParams(
            collective_id=name, has_side_effects=True, vmem_limit_bytes=62 << 20
        ),
        name="front",
    )(pairing, lengths, *vectors, tokens, cotangent, w_qkv, w_out, w_in, w_back)


PARTS = 12


def sum_sources(chunk):
    left = jnp.where(chunk < 4, 3 + chunk, jnp.where(chunk < 8, 2, jnp.where(chunk < 9, 1, 0)))
    right = jnp.where(
        chunk < 4, 8, jnp.where(chunk < 8, chunk, jnp.where(chunk < 9, 3, chunk - 9))
    )
    return left, right


STEPS = 65
PLAN = {
    "pair": {0: 0, 1: 1, 2: 2, 3: 3, 6: 4, 7: 5, 13: 6, 15: 7, 19: 8, 21: 9, 29: 10, 32: 11},
    "x": {3: 0, 4: 1, 5: 2, 7: 3, 12: 4, 13: 5, 14: 6, 18: 7, 23: 8, 30: 9, 36: 10, 41: 11},
    "y": {9: 0, 10: 1, 16: 2, 17: 3, 18: 4, 21: 5, 24: 6, 26: 7, 30: 8, 36: 9, 46: 10, 50: 11},
    "near": {11: 0, 19: 1, 20: 2, 24: 3, 25: 4, 28: 5, 32: 6, 38: 7, 42: 8, 44: 9, 49: 10, 57: 11},
    "far": {22: 0, 25: 1, 26: 2, 31: 3, 33: 4, 39: 5, 41: 6, 44: 7, 47: 8, 52: 9, 55: 10, 60: 11},
    "own": {27: 0, 29: 1, 30: 2, 37: 3, 40: 4, 45: 5, 49: 6, 50: 7, 53: 8, 57: 9, 58: 10, 61: 11},
    "wide": {30: 0, 31: 1, 34: 2, 43: 3, 48: 4, 50: 5, 51: 6, 56: 7, 57: 8, 59: 9, 61: 10, 62: 11},
    "last": {35: 0, 38: 1, 42: 2, 47: 3, 52: 4, 54: 5, 55: 6, 58: 7, 60: 8, 61: 9, 63: 10, 64: 11},
}
ATTEND_AT = (8, 9, 10)
JOIN_AT = (16, 24, 28)
SMALL_AT = (46, 49, 52, 61, 62, 64)
TOKEN_AT = 44


def planned(name, step):
    chunk = jnp.int32(-1)
    for at, which in PLAN[name].items():
        chunk = jnp.where(step == at, which, chunk)
    return chunk


def back_kernel(
    n, pair_ref, len_ref, grad_ref, keep_src, mix_src, lse_src, left_src, right_src,
    sums_src, resid_src, qkv_ref,
    total_out, token_ref, small_out,
    keep_ref, mix_ref, lse_ref, left_ref, sums_ref, resid_ref, total_ref,
    grad_in, g_all, q_sum, k_sum, v_sum, folded_out, folded_in,
    blocks_out, blocks_in, w_qkv, right_all,
    pair_out, pair_in, x_out, x_in, y_out, y_in, y_keep, near_out, near_in, near_keep,
    far_out, far_in, far_keep, s_out, s_in,
    load_sem, ship_sem,
    grad_sem, block_q, block_k, block_v, own_sem, pair_sem, x_sem, y_sem, near_sem, far_sem,
    own_z_sem, wide_sem, last_sem, s_sem,
):
    block_sem = (block_q, block_k, block_v)
    low, wide = jnp.bfloat16, jnp.float32
    ctx = lax.axis_index("ctx")
    fsdp = lax.axis_index("fsdp")
    z, y = ctx // 2, lax.rem(ctx, 2)
    odd, upper = lax.rem(z, 2), z // 2
    x, core = fsdp // 2, lax.rem(fsdp, 2)
    sibling = {"fsdp": 2 * x + 1 - core}
    across = {"fsdp": 2 * (1 - x) + core}
    over_y = {"ctx": 2 * z + 1 - y}
    near = {"ctx": 2 * (2 * upper + 1 - odd) + y}
    far = {"ctx": 2 * (2 * (1 - upper) + odd) + y}
    mine = 2 * odd + upper
    loads = [
        pltpu.make_async_copy(src, dst, load_sem.at[i])
        for i, (src, dst) in enumerate(
            [
                (right_src, right_all.at[3:]),
                (left_src, left_ref),
                (keep_src, keep_ref),
                (mix_src, mix_ref),
                (lse_src, lse_ref),
                (sums_src, sums_ref),
                (resid_src, resid_ref),
            ]
        )
    ]
    for cp in loads:
        cp.start()
    greet(ring_peers(n) + [sibling, across])
    lead = lax.rem(pair_ref[2 * ctx], 2)
    grads = exchange_copies(n, grad_ref, grad_in, grad_sem, one)
    for cp in grads:
        cp.start()
    own_grad = own_copy(grad_ref, grad_in, own_sem.at[0], one)
    own_grad.start()
    load = pltpu.make_async_copy(qkv_ref, w_qkv, own_sem.at[1])
    load.start()
    blocks = [
        exchange_copies(n, folded_out, folded_in, block_sem[0], one)
    ] + [
        exchange_copies(n, blocks_out.at[p], blocks_in.at[p], block_sem[1 + p])
        for p in range(2)
    ]
    own = [own_copy(folded_out, folded_in, own_sem.at[2], one)] + [
        own_copy(blocks_out.at[p], blocks_in.at[p], own_sem.at[3 + p]) for p in range(2)
    ]
    k_sum[...] = jnp.zeros_like(k_sum)
    v_sum[...] = jnp.zeros_like(v_sum)
    chunks = keep_ref.shape[1] // 2

    def attend_some(first, last):
        for c in range(first, last):
            attend_back(
                c, len_ref[0], y, keep_ref, g_all, mix_ref, lse_ref, q_sum, k_sum, v_sum
            )

    def attend_step(t):
        @pl.when(t == ATTEND_AT[0])
        def _():
            own_grad.wait()
            for cp in loads[2:5]:
                cp.wait()
            for cp in grads:
                cp.wait_recv()
            for b in range(2 * chunks):
                found = spot_of(pair_ref, b)
                g_all[b] = unfold_block(grad_in[lax.div(found, 2)], lax.rem(found, 2))
            attend_some(0, chunks // 2)

        @pl.when(t == ATTEND_AT[1])
        def _():
            attend_some(chunks // 2, chunks - 2)

        @pl.when(t == ATTEND_AT[2])
        def _():
            attend_some(chunks - 2, chunks)
            for peer in range(n):
                first, second = q_sum[pair_ref[2 * peer]], q_sum[pair_ref[2 * peer + 1]]
                folded_out[peer] = fold(
                    first, second, first[:, HEAD_DIM:] + second[:, HEAD_DIM:]
                ).astype(low)
            for p, total in enumerate((None, k_sum, v_sum)):
                if p:
                    for s in range(2 * chunks):
                        blocks_out[p - 1, s] = total[pair_ref[s]].astype(low)
                for cp in blocks[p]:
                    cp.start()
                own[p].start()

    def slot(c):
        return lax.rem(c, 4)

    def pair_copy(c):
        return remote(pair_out.at[lax.rem(c, 2)], pair_in.at[c], pair_sem, (c,), sibling)

    def x_copy(c):
        return remote(x_out.at[c], x_in.at[c], x_sem, (c,), across)

    def y_copy(c):
        return remote(y_out.at[slot(c)], y_in.at[c], y_sem, (c,), over_y)

    def near_copy(c):
        return remote(near_out.at[slot(c)], near_in.at[c], near_sem, (c,), near)

    def far_copy(c):
        return remote(far_out.at[slot(c)], far_in.at[c], far_sem, (c,), far)

    def own_z_copy(c):
        piece = total_ref.at[c, y, mine]
        return remote(piece, piece, own_z_sem, (c,), far)

    def wide_copy(c):
        piece = total_ref.at[c, y, two(odd)]
        return remote(piece, piece, wide_sem, (c,), near)

    def last_copy(c):
        piece = total_ref.at[c, y]
        return remote(piece, piece, last_sem, (c,), over_y)

    def reuse(copy, c, slots):
        @pl.when(c >= slots)
        def _():
            copy(c - slots).wait_send()

    def partial(c, shard):
        left, right = sum_sources(c)
        return dot_nn(left_ref[left, shard], right_all[right])

    def stage_pair(c):
        reuse(pair_copy, c, 2)
        for side in range(2):
            pair_out[lax.rem(c, 2), side] = partial(c, 2 * side + 1 - core).astype(low)
        pair_copy(c).start()

    def stage_x(c):
        pair_copy(c).wait_recv()
        x_out[c] = (partial(c, 2 * (1 - x) + core) + pair_in[c, 1 - x].astype(wide)).astype(low)
        x_copy(c).start()

    def stage_y(c):
        mine_sum = partial(c, 2 * x + core) + pair_in[c, x].astype(wide)
        x_copy(c).wait_recv()
        total = mine_sum + x_in[c].astype(wide)
        first, second = total[:, :384], total[:, 384:]
        reuse(y_copy, c, 4)
        y_out[slot(c)] = jnp.where(y == 0, second, first).astype(low)
        y_copy(c).start()
        y_keep[slot(c)] = jnp.where(y == 0, first, second)

    def stage_near(c):
        y_copy(c).wait_recv()
        total = y_keep[slot(c)] + y_in[c].astype(wide)
        first, second = total[:96], total[96:]
        reuse(near_copy, c, 4)
        near_out[slot(c)] = jnp.where(odd == 0, second, first).astype(low)
        near_copy(c).start()
        near_keep[slot(c)] = jnp.where(odd == 0, first, second)

    def stage_far(c):
        near_copy(c).wait_recv()
        total = near_keep[slot(c)] + near_in[c].astype(wide)
        first, second = total[:48], total[48:]
        reuse(far_copy, c, 4)
        far_out[slot(c)] = jnp.where(upper == 0, second, first).astype(low)
        far_copy(c).start()
        far_keep[slot(c)] = jnp.where(upper == 0, first, second)

    def stage_own(c):
        far_copy(c).wait_recv()
        total_ref[c, y, mine] = (far_keep[slot(c)] + far_in[c].astype(wide)).astype(low)
        own_z_copy(c).start()

    def stage_wide(c):
        own_z_copy(c).wait_recv()
        wide_copy(c).start()

    def stage_last(c):
        wide_copy(c).wait_recv()
        last_copy(c).start()

    def small_step(t):
        peers = [sibling, across, over_y, near, far]
        copies = [
            remote(s_out.at[k], s_in.at[k], s_sem, (k,), peer) for k, peer in enumerate(peers)
        ]

        for p in range(3):

            @pl.when(t == JOIN_AT[p])
            def _():
                own[p].wait()
                for cp in blocks[p]:
                    cp.wait_recv()
                if p:
                    right_all[p] = join_pairs(lambda peer: both(blocks_in.at[p - 1], peer))
                else:
                    right_all[p] = join_folded(lambda peer: folded_in[peer], lead)

        @pl.when(t == SMALL_AT[0])
        def _():
            loads[5].wait()
            s_out[0] = sums_ref[...]
            s_out[0, ROW_BQ : ROW_BQ + 1] = column_sum(right_all[0].astype(wide))
            s_out[0, ROW_BV : ROW_BV + 1] = column_sum(right_all[2].astype(wide))
            copies[0].start()

        for k in range(1, 5):

            @pl.when(t == SMALL_AT[k])
            def _():
                copies[k - 1].wait()
                s_out[k] = s_out[k - 1] + s_in[k - 1]
                copies[k].start()

        @pl.when(t == SMALL_AT[5])
        def _():
            copies[4].wait()
            total = s_out[4] + s_in[4]
            quarter = total.shape[1] // 4
            cuts = [slice(f * quarter, (f + 1) * quarter) for f in range(4)]
            pick = lambda choices: sum(
                jnp.where(fsdp == f, choice, 0.0) for f, choice in enumerate(choices)
            )
            small_out[...] = jnp.zeros_like(small_out)
            small_out[:8] = pick([total[:8, cut] for cut in cuts])
            line = pick([total[ROW_BI + f : ROW_BI + f + 1] for f in range(4)])
            for j, cut in enumerate(cuts):
                small_out[8 + j : 9 + j] = line[:, cut]

        @pl.when(t == TOKEN_AT)
        def _():
            load.wait()
            loads[6].wait()
            width = resid_ref.shape[1]
            token_ref[...] = resid_ref[...] + sum(
                dot_nt(
                    right_all[part],
                    w_qkv[:, :, part * width : (part + 1) * width].reshape(width, width),
                )
                for part in range(3)
            )

    stages = [
        ("pair", stage_pair),
        ("x", stage_x),
        ("last", stage_last),
        ("wide", stage_wide),
        ("own", stage_own),
        ("far", stage_far),
        ("near", stage_near),
        ("y", stage_y),
    ]

    def step(t, carry):
        attend_step(t)
        small_step(t)
        for name, stage in stages:
            c = planned(name, t)

            @pl.when(c >= 0)
            def _():
                stage(c)

        return carry

    loads[0].wait()
    loads[1].wait()
    lax.fori_loop(0, STEPS, step, 0)

    def ship(c):
        return pltpu.make_async_copy(total_ref.at[c], total_out.at[c], ship_sem.at[c])

    def drain(c, carry):
        x_copy(c).wait_send()
        own_z_copy(c).wait_send()
        wide_copy(c).wait_send()
        last_copy(c).wait()
        ship(c).start()
        return carry

    lax.fori_loop(0, PARTS, drain, 0)
    for c in range(PARTS - 4, PARTS):
        y_copy(c).wait_send()
        near_copy(c).wait_send()
        far_copy(c).wait_send()
    for c in (PARTS - 2, PARTS - 1):
        pair_copy(c).wait_send()
    for cp in grads + blocks[0] + blocks[1] + blocks[2]:
        cp.wait_send()
    for c in range(PARTS):
        ship(c).wait()


def back(pairing, lengths, grad, keep, mix, lse, left, right, sums, resid, qkv_full, name):
    blocks = keep.shape[1]
    n = blocks // 2
    low, wide = jnp.bfloat16, jnp.float32
    dma = pltpu.SemaphoreType.DMA
    shape = jax.ShapeDtypeStruct
    total = pltpu.VMEM((blocks, BLK, BLK), wide)
    hbm = pl.BlockSpec(memory_space=pltpu.HBM)
    return pl.pallas_call(
        functools.partial(back_kernel, n),
        out_shape=(
            shape((PARTS, 2, 4, 48, 384), low),
            shape(resid.shape, wide),
            shape((16, 192), wide),
        ),
        in_specs=[smem()] * 2 + [hbm] * 9,
        out_specs=(hbm, vmem(), vmem()),
        scratch_shapes=[
            pltpu.VMEM(keep.shape, low),
            pltpu.VMEM(mix.shape, wide),
            pltpu.VMEM(lse.shape, wide),
            pltpu.VMEM(left.shape, low),
            pltpu.VMEM(sums.shape, wide),
            pltpu.VMEM(resid.shape, wide),
            pltpu.VMEM((PARTS, 2, 4, 48, 384), low),
            pltpu.VMEM(grad.shape, low),
            pltpu.VMEM((blocks, BLK, BLK), low),
            total, total, total,
            pltpu.VMEM(grad.shape, low),
            pltpu.VMEM(grad.shape, low),
            pltpu.VMEM((2, blocks, BLK, BLK), low),
            pltpu.VMEM((2, blocks, BLK, BLK), low),
            pltpu.VMEM(qkv_full.shape, low),
            pltpu.VMEM((9,) + right.shape[1:], low),
            pltpu.VMEM((2, 2, 192, 768), low),
            pltpu.VMEM((PARTS, 2, 192, 768), low),
            pltpu.VMEM((PARTS, 192, 768), low),
            pltpu.VMEM((PARTS, 192, 768), low),
            pltpu.VMEM((4, 192, 384), low),
            pltpu.VMEM((PARTS, 192, 384), low),
            pltpu.VMEM((4, 192, 384), wide),
            pltpu.VMEM((4, 96, 384), low),
            pltpu.VMEM((PARTS, 96, 384), low),
            pltpu.VMEM((4, 96, 384), wide),
            pltpu.VMEM((4, 48, 384), low),
            pltpu.VMEM((PARTS, 48, 384), low),
            pltpu.VMEM((4, 48, 384), wide),
            pltpu.VMEM((5,) + sums.shape, wide),
            pltpu.VMEM((5,) + sums.shape, wide),
            dma((7,)),
            dma((PARTS,)),
            dma((2, n)),
            dma((2, n)),
            dma((2, n)),
            dma((2, n)),
            dma((5,)),
        ]
        + [dma((2, PARTS))] * 8
        + [dma((2, 5))],
        compiler_params=pltpu.CompilerParams(
            collective_id=name, has_side_effects=True, vmem_limit_bytes=61 << 20
        ),
        name="back",
    )(pairing, lengths, grad, keep, mix, lse, left, right, sums, resid, qkv_full)


def finish_kernel(
    total_ref, small_ref, output_ref, token_ref,
    output_out, token_out, qkv_out, out_out, in_out, back_out, *refs
):
    lines, (total, small, through, stage, sems) = refs[:9], refs[9:]
    arrive = [
        pltpu.make_async_copy(total_ref.at[c], total.at[c], sems.at[PARTS + 2 + c])
        for c in range(PARTS)
    ] + [
        pltpu.make_async_copy(small_ref, small, sems.at[2 * PARTS + 2]),
        pltpu.make_async_copy(output_ref, through.at[0], sems.at[2 * PARTS + 3]),
        pltpu.make_async_copy(token_ref, through.at[1], sems.at[2 * PARTS + 4]),
    ]
    for cp in arrive:
        cp.start()
    copies = [
        pltpu.make_async_copy(through.at[0], output_out, sems.at[PARTS]),
        pltpu.make_async_copy(through.at[1], token_out, sems.at[PARTS + 1]),
    ]
    targets = [back_out.at[192 * k : 192 * k + 192] for k in range(4)]
    targets += [in_out.at[:, 768 * k : 768 * k + 768] for k in range(4)]
    targets += [out_out]
    targets += [qkv_out.at[:, 768 * k : 768 * k + 768] for k in range(3)]
    for c, target in enumerate(targets):
        arrive[c].wait()
        for half in range(2):
            for spot in range(4):
                stage[c, 48 * spot : 48 * spot + 48, 384 * half : 384 * half + 384] = total[
                    c, half, spot
                ].astype(jnp.float32)
        copies.append(pltpu.make_async_copy(stage.at[c], target, sems.at[c]))
        copies[-1].start()
    for k in range(2):
        arrive[PARTS + 1 + k].wait()
        copies[k].start()
    arrive[PARTS].wait()
    for i in range(8):
        lines[i][...] = small[i]
    for j in range(4):
        lines[8][192 * j : 192 * j + 192] = small[ROW_BI + j]
    for cp in copies:
        cp.wait()


def finish(total, small, output, token):
    shape = jax.ShapeDtypeStruct
    wide = jnp.float32
    hbm = pl.BlockSpec(memory_space=pltpu.HBM)
    return pl.pallas_call(
        finish_kernel,
        out_shape=(
            shape(output.shape, wide),
            shape(token.shape, wide),
            shape((192, 2304), wide),
            shape((192, 768), wide),
            shape((192, 3072), wide),
            shape((768, 768), wide),
        )
        + (shape((192,), wide),) * 8
        + (shape((768,), wide),),
        in_specs=[hbm] * 4,
        out_specs=(hbm,) * 6 + (vmem(),) * 9,
        scratch_shapes=[
            pltpu.VMEM(total.shape, total.dtype),
            pltpu.VMEM(small.shape, wide),
            pltpu.VMEM((2,) + token.shape, wide),
            pltpu.VMEM((PARTS, 192, 768), wide),
            pltpu.SemaphoreType.DMA((2 * PARTS + 5,)),
        ],
        compiler_params=pltpu.CompilerParams(vmem_limit_bytes=62 << 20),
        name="finish",
    )(total, small, output, token)


def on_device_spread(
    tokens,
    cotangent,
    lengths,
    pairing,
    w_qkv,
    bias_q,
    bias_v,
    w_out,
    bias_out,
    ln1_gain,
    ln1_bias,
    w_in,
    bias_in,
    w_back,
    bias_back,
    ln2_gain,
    ln2_bias,
):
    n = pairing.shape[0] // 2
    inputs = tokens[0]
    vectors = [bias_q, bias_v, bias_out, ln1_gain, ln1_bias, bias_back, ln2_gain, ln2_bias]
    vectors += [bias_in]
    output, grad, left, right, resid, sums, keep, mix, lse, qkv_full = front(
        pairing, lengths, vectors, inputs, cotangent[0], w_qkv, w_out, w_in, w_back, n, 0
    )
    total, token_grad, small_sum = back(
        pairing, lengths, grad, keep, mix, lse, left, right, sums, resid, qkv_full, 1
    )
    (
        output, token_grad, qkv_sum, out_sum, in_sum, back_sum,
        bq, bv, bo, g1, s1, bb, g2, s2, bi,
    ) = finish(total, small_sum, output, token_grad)
    return (
        output[None], token_grad[None], qkv_sum, bq, bv, out_sum, bo, g1, s1, in_sum, bi,
        back_sum, bb, g2, s2,
    )


def solution(mesh):
    return jax.shard_map(
        on_device_spread if mesh.shape["ctx"] == 8 else on_device_any,
        mesh=mesh,
        in_specs=(
            P("fsdp", "ctx", None),
            P("fsdp", "ctx", None),
            P("fsdp"),
            P(),
            P("fsdp", None),
            P("fsdp"),
            P("fsdp"),
            P("fsdp", None),
            P("fsdp"),
            P("fsdp"),
            P("fsdp"),
            P("fsdp", None),
            P("fsdp"),
            P("fsdp", None),
            P("fsdp"),
            P("fsdp"),
            P("fsdp"),
        ),
        out_specs=(
            P("fsdp", "ctx", None),
            P("fsdp", "ctx", None),
            P("fsdp", None),
            P("fsdp"),
            P("fsdp"),
            P("fsdp", None),
            P("fsdp"),
            P("fsdp"),
            P("fsdp"),
            P("fsdp", None),
            P("fsdp"),
            P("fsdp", None),
            P("fsdp"),
            P("fsdp"),
            P("fsdp"),
        ),
        check_vma=False,
    )
```

profile of v0, /device:TPU:0, one launch (start us, length us, event | category | flops | bytes accessed | tf_op | source)
XLA Modules:
  0.0 216.3 jit_solution(2703963014533839034)
XLA Ops:
  1.3 81.1 %front.1 = (f32[256,768]{1,0:T(8,128)}, bf16[8,192,128]{2,1,0:T(8,128)(2,1)}, bf16[7,4,192,256]{3,2,1,0:T(8,128)(2,1)}, bf16[6,256,768]{2,1,0:T(8,128)(2,1)}, f3...) custom-call(s32[16]{0:T(128)} %pair_ref.3, ...), custom_call_target="tpu_custom_call" | custom-call | tf_op jit(solution)/shard_map/front/pallas_call | solution.py:1015
  82.4 128.1 %back.1 = (bf16[12,2,4,48,384]{4,3,2,1,0:T(8,128)(2,1)}, f32[256,768]{1,0:T(8,128)}, f32[16,192]{1,0:T(8,128)}) custom-call(s32[16]{0:T(128)} %pair_ref.3, s32[1]{0:T(128)S(6)} %copy.32.len_ref, bf16[8,192,128]{2,1,0:T(8,128)(2,1)} %get-tuple-element.43.grad_ref, bf16[3,16,128,128]{3,2,1,0:T(8,128)(2,1)} %get-tuple-element.44.keep_src, ...), custom_call_target="tpu_custom_call" | custom-call | tf_op jit(solution)/shard_map/back/pallas_call | solution.py:1419
  210.6 5.5 %finish.1 = (f32[256,768]{1,0:T(8,128)}, f32[256,768]{1,0:T(8,128)}, f32[192,2304]{1,0:T(8,128)}, f32[192,768]{1,0:T(8,128)}, f32[192,3072]{1,0:T(8,128)}, /*ind...) custom-call(bf16[12,2,4,48,384]{4,3,2,1,0:T(8,128)(2,1)} %get-tuple-, ...), custom_call_target="tpu_custom_call" | custom-call | tf_op jit(solution)/shard_map/finish/pallas_call | solution.py:1525
where the time goes:
time: 216 us
  Pallas kernels  215 us (100%)
    pallas_call x1, Pallas kernels, back(): pl.pallas_call(functools.partial(back_kernel, n), out_shape=(shape((PARTS...  128 us
    pallas_call x1, Pallas kernels, front(): pl.pallas_call(functools.partial(front_kernel, n), out_shape=tuple((shape...  81.1 us
    pallas_call x1, Pallas kernels, finish(): pl.pallas_call(finish_kernel, out_shape=(shape(output.shape, wide), shape...  5.53 us

commit v1 on v0

--- a/solution.py
+++ b/solution.py
@@ -799,7 +799,7 @@
         small_out[8 + j : 9 + j] = inner_bias[:, j * part : (j + 1) * part]
     greet(ring_peers(n) + chip_peers())
     smalls = gather_copies(small_out, small, small_sem, 0)
-    qkv_split = split_gather(qkv_src, w_qkv, qkv_sem, 3)
+    qkv_split = split_gather(qkv_src, w_qkv, qkv_sem, 6)
     in_split = split_gather(in_src, w_in, in_split_sem, count)
     back_split = split_gather(back_src, w_back, back_split_sem, 2)
     splits = (qkv_split, in_split, back_split)
@@ -814,6 +814,7 @@
     smalls[0].wait_recv()
     smalls[2].start()
     passed(qkv_split, 0)
+    passed(qkv_split, 1)
     loads[0].wait()
     tokens = token_buf[...]
     left[0] = jnp.transpose(tokens).reshape(4, -1, 2 * BLK)
@@ -828,9 +829,11 @@
             ]
     rows_ref[12:] = jnp.zeros_like(rows_ref[12:])
     row = lambda i: rows_ref[i : i + 1, :]
-    passed(qkv_split, 1)
     handed(qkv_split, 0)
     passed(qkv_split, 2)
+    handed(qkv_split, 1)
+    for p in range(3, 6):
+        passed(qkv_split, p)
     for cp in shards[:2]:
         cp.start()
     for split in (in_split, back_split):
@@ -839,9 +842,10 @@
     loads[2].wait()
     sends = []
     for p, bias in enumerate((ROW_BQ, None, ROW_BV)):
-        if p:
-            handed(qkv_split, p)
-        gathered(qkv_split, p)
+        for q in (2 * p, 2 * p + 1):
+            if p:
+                handed(qkv_split, q)
+            gathered(qkv_split, q)
         value = dot_nn(tokens, w_qkv[:, :, p * width : (p + 1) * width].reshape(width, width))
         if bias is not None:
             value = value + row(bias)
@@ -893,11 +897,12 @@
                 keep[p, b] = unfold_block(
                     packed[p][lax.div(spots_of[b], 2)], lax.rem(spots_of[b], 2)
                 )
-    passed(back_split, 1)
 
     ship(keep, keep_ref)
     for c in range(n):
         attend(c, len_ref[0], spot, keep, mix, lse, turned)
+        if c == 0:
+            passed(back_split, 1)
     for peer in range(n):
         first, second = turned[pair_ref[2 * peer]], turned[pair_ref[2 * peer + 1]]
         mixed_out[peer] = fold(first, second, first[:, HEAD_DIM:] + second[:, HEAD_DIM:])
@@ -1047,7 +1052,7 @@
             resid,
             sums,
             dma((2, 1, 3)),
-            dma((2, 5, 3)),
+            dma((2, 5, 6)),
             dma((2, 5, 4)),
             dma((2, 5, 2)),
             dma((2, 1, 3)),
@@ -1104,8 +1109,8 @@
 def back_kernel(
     n, pair_ref, len_ref, grad_ref, keep_src, mix_src, lse_src, left_src, right_src,
     sums_src, resid_src, qkv_ref,
-    total_out, token_ref, small_out,
-    keep_ref, mix_ref, lse_ref, left_ref, sums_ref, resid_ref, total_ref,
+    total_out, token_out, small_dst,
+    token_ref, small_out, keep_ref, mix_ref, lse_ref, left_ref, sums_ref, resid_ref, total_ref,
     grad_in, g_all, q_sum, k_sum, v_sum, folded_out, folded_in,
     blocks_out, blocks_in, w_qkv, right_all,
     pair_out, pair_in, x_out, x_in, y_out, y_in, y_keep, near_out, near_in, near_keep,
@@ -1295,6 +1300,9 @@
         wide_copy(c).wait_recv()
         last_copy(c).start()
 
+    token_ship = pltpu.make_async_copy(token_ref, token_out, ship_sem.at[PARTS])
+    small_ship = pltpu.make_async_copy(small_out, small_dst, ship_sem.at[PARTS + 1])
+
     def small_step(t):
         peers = [sibling, across, over_y, near, far]
         copies = [
@@ -1343,6 +1351,7 @@
             line = pick([total[ROW_BI + f : ROW_BI + f + 1] for f in range(4)])
             for j, cut in enumerate(cuts):
                 small_out[8 + j : 9 + j] = line[:, cut]
+            small_ship.start()
 
         @pl.when(t == TOKEN_AT)
         def _():
@@ -1356,6 +1365,7 @@
                 )
                 for part in range(3)
             )
+            token_ship.start()
 
     stages = [
         ("pair", stage_pair),
@@ -1406,6 +1416,8 @@
         cp.wait_send()
     for c in range(PARTS):
         ship(c).wait()
+    token_ship.wait()
+    small_ship.wait()
 
 
 def back(pairing, lengths, grad, keep, mix, lse, left, right, sums, resid, qkv_full, name):
@@ -1424,8 +1436,10 @@
             shape((16, 192), wide),
         ),
         in_specs=[smem()] * 2 + [hbm] * 9,
-        out_specs=(hbm, vmem(), vmem()),
+        out_specs=(hbm,) * 3,
         scratch_shapes=[
+            pltpu.VMEM(resid.shape, wide),
+            pltpu.VMEM((16, 192), wide),
             pltpu.VMEM(keep.shape, low),
             pltpu.VMEM(mix.shape, wide),
             pltpu.VMEM(lse.shape, wide),
@@ -1458,7 +1472,7 @@
             pltpu.VMEM((5,) + sums.shape, wide),
             pltpu.VMEM((5,) + sums.shape, wide),
             dma((7,)),
-            dma((PARTS,)),
+            dma((PARTS + 2,)),
             dma((2, n)),
             dma((2, n)),
             dma((2, n)),

time: 216 us -> 215 us (level)
  no operation moved by 1% of the time
where the time goes in v1:
time: 215 us; the launch traced here: 214 us
  Pallas kernels  213 us (99%)
    pallas_call x1, Pallas kernels, back(): pl.pallas_call(functools.partial(back_kernel, n), out_shape=(shape((PARTS...  127 us
    pallas_call x1, Pallas kernels, front(): pl.pallas_call(functools.partial(front_kernel, n), out_shape=tuple((shape...  80.5 us
    pallas_call x1, Pallas kernels, finish(): pl.pallas_call(finish_kernel, out_shape=(shape(output.shape, wide), shape...  5.53 us

profile of v1, /device:TPU:0, one launch (start us, length us, event | category | flops | bytes accessed | tf_op | source)
XLA Modules:
  0.0 214.4 jit_solution(9327363482594349737)
XLA Ops:
  1.3 80.5 %front.1 = (f32[256,768]{1,0:T(8,128)}, bf16[8,192,128]{2,1,0:T(8,128)(2,1)}, bf16[7,4,192,256]{3,2,1,0:T(8,128)(2,1)}, bf16[6,256,768]{2,1,0:T(8,128)(2,1)}, f3...) custom-call(s32[16]{0:T(128)} %pair_ref.3, ...), custom_call_target="tpu_custom_call" | custom-call | tf_op jit(solution)/shard_map/front/pallas_call | solution.py:1020
  81.8 126.8 %back.1 = (bf16[12,2,4,48,384]{4,3,2,1,0:T(8,128)(2,1)}, f32[256,768]{1,0:T(8,128)}, f32[16,192]{1,0:T(8,128)}) custom-call(s32[16]{0:T(128)} %pair_ref.3, s32[1]{0:T(128)S(6)} %copy.32.len_ref, bf16[8,192,128]{2,1,0:T(8,128)(2,1)} %get-tuple-element.43.grad_ref, bf16[3,16,128,128]{3,2,1,0:T(8,128)(2,1)} %get-tuple-element.44.keep_src, ...), custom_call_target="tpu_custom_call" | custom-call | tf_op jit(solution)/shard_map/back/pallas_call | solution.py:1431
  208.7 5.5 %finish.1 = (f32[256,768]{1,0:T(8,128)}, f32[256,768]{1,0:T(8,128)}, f32[192,2304]{1,0:T(8,128)}, f32[192,768]{1,0:T(8,128)}, f32[192,3072]{1,0:T(8,128)}, /*ind...) custom-call(bf16[12,2,4,48,384]{4,3,2,1,0:T(8,128)(2,1)} %get-tuple-, ...), custom_call_target="tpu_custom_call" | custom-call | tf_op jit(solution)/shard_map/finish/pallas_call | solution.py:1539

commit v2 on v1

--- a/solution.py
+++ b/solution.py
@@ -563,11 +563,15 @@
     )
 
 
-def greet(peers):
+def hail(peers):
     barrier = pltpu.get_barrier_semaphore()
     for peer in peers:
         pl.semaphore_signal(barrier, inc=1, device_id=peer, device_id_type=MESH)
-    pl.semaphore_wait(barrier, len(peers))
+
+
+def greet(peers):
+    hail(peers)
+    pl.semaphore_wait(pltpu.get_barrier_semaphore(), len(peers))
 
 
 def ring_peers(n):
@@ -788,6 +792,8 @@
         )
     ]
     cot_load = loads[1]
+    peers = ring_peers(n) + chip_peers()
+    hail(peers)
     for cp in loads[:3]:
         cp.start()
     part = width // 4
@@ -797,15 +803,16 @@
     inner_bias = vectors[8][...].astype(wide).reshape(1, -1)
     for j in range(4):
         small_out[8 + j : 9 + j] = inner_bias[:, j * part : (j + 1) * part]
-    greet(ring_peers(n) + chip_peers())
+    pl.semaphore_wait(pltpu.get_barrier_semaphore(), len(peers))
     smalls = gather_copies(small_out, small, small_sem, 0)
     qkv_split = split_gather(qkv_src, w_qkv, qkv_sem, 6)
     in_split = split_gather(in_src, w_in, in_split_sem, count)
     back_split = split_gather(back_src, w_back, back_split_sem, 2)
     splits = (qkv_split, in_split, back_split)
+    qkv_split[0][0].start()
     for step in (0, 1):
         smalls[step].start()
-    for cp in qkv_split[0] + qkv_split[4]:
+    for cp in qkv_split[0][1:] + qkv_split[4]:
         cp.start()
     for cp in loads[3:]:
         cp.start()

time: 215 us -> 214 us (level)
  no operation moved by 1% of the time
where the time goes in v2:
time: 214 us; the launch traced here: 213 us
  Pallas kernels  211 us (99%)
    pallas_call x1, Pallas kernels, back(): pl.pallas_call(functools.partial(back_kernel, n), out_shape=(shape((PARTS...  125 us
    pallas_call x1, Pallas kernels, front(): pl.pallas_call(functools.partial(front_kernel, n), out_shape=tuple((shape...  80.6 us
    pallas_call x1, Pallas kernels, finish(): pl.pallas_call(finish_kernel, out_shape=(shape(output.shape, wide), shape...  5.53 us

profile of v2, /device:TPU:0, one launch (start us, length us, event | category | flops | bytes accessed | tf_op | source)
XLA Modules:
  0.0 212.7 jit_solution(9489901639533707687)
XLA Ops:
  1.3 80.6 %front.1 = (f32[256,768]{1,0:T(8,128)}, bf16[8,192,128]{2,1,0:T(8,128)(2,1)}, bf16[7,4,192,256]{3,2,1,0:T(8,128)(2,1)}, bf16[6,256,768]{2,1,0:T(8,128)(2,1)}, f3...) custom-call(s32[16]{0:T(128)} %pair_ref.3, ...), custom_call_target="tpu_custom_call" | custom-call | tf_op jit(solution)/shard_map/front/pallas_call | solution.py:1027
  81.9 125.1 %back.1 = (bf16[12,2,4,48,384]{4,3,2,1,0:T(8,128)(2,1)}, f32[256,768]{1,0:T(8,128)}, f32[16,192]{1,0:T(8,128)}) custom-call(s32[16]{0:T(128)} %pair_ref.3, s32[1]{0:T(128)S(6)} %copy.32.len_ref, bf16[8,192,128]{2,1,0:T(8,128)(2,1)} %get-tuple-element.43.grad_ref, bf16[3,16,128,128]{3,2,1,0:T(8,128)(2,1)} %get-tuple-element.44.keep_src, ...), custom_call_target="tpu_custom_call" | custom-call | tf_op jit(solution)/shard_map/back/pallas_call | solution.py:1438
  206.9 5.5 %finish.1 = (f32[256,768]{1,0:T(8,128)}, f32[256,768]{1,0:T(8,128)}, f32[192,2304]{1,0:T(8,128)}, f32[192,768]{1,0:T(8,128)}, f32[192,3072]{1,0:T(8,128)}, /*ind...) custom-call(bf16[12,2,4,48,384]{4,3,2,1,0:T(8,128)(2,1)} %get-tuple-, ...), custom_call_target="tpu_custom_call" | custom-call | tf_op jit(solution)/shard_map/finish/pallas_call | solution.py:1546
